TPU v7x, 32 devices: a whole 2x2x4 slice. The times are simulated.
32 devices in a mesh: groups: 2 (over y), rows: 4 (over x, core), cols: 4 (over z).
Axes of the slice: x: 2, y: 2, z: 4, core: 2. Of those that a mesh axis runs over, the one named last changes fastest.
Arguments:
- source_emb: bfloat16 [8192, 256], P(('groups', 'rows', 'cols')), parts along dimension 0, may hold values from -400 to 400
- target_emb: bfloat16 [8192, 256], P(('groups', 'cols', 'rows')), parts along dimension 0, may hold values from -400 to 400
- source_mass: float32 [8192], P(('groups', 'rows', 'cols')), parts along dimension 0, may hold values from 0.25 to 4
- target_mass: float32 [8192], P(('groups', 'cols', 'rows')), parts along dimension 0, may hold values from 0.25 to 4
- cand_cols: int32 [64, 16], P(('groups', 'rows'), 'cols'), parts along dimension 0, may hold values from 0 to 7, as said below
- cand_count: int32 [64, 4], P(('groups', 'rows'), 'cols'), parts along dimension 0, may hold values from 1 to 4, as said below
Outputs:
- source_potential: float32 [8192], P(('groups', 'rows', 'cols')), parts along dimension 0
- target_potential: float32 [8192], P(('groups', 'cols', 'rows')), parts along dimension 0
There are 2 independent parts, one for each index of `groups`. A program takes and returns all parts, laid end to end along the dimension named above; each array names one. Nothing has to cross between parts.
Inputs may be any that keep to these rules, and one draw needn't show every extreme that they name: `cand_cols`: entries c * 4 to c * 4 + 3 of row s are distinct local numbers of target blocks of column group c; only the first cand_count[s, c] of them are pairs. Within each row group and column group, the first entries of every 8 consecutive source blocks name each of the group's 8 target blocks once. `cand_count`: in every row group and column group some source block has 4 candidate blocks.
All inputs are finite; a program needn't handle non-finite values.
Results may differ from a plain program's by a relative error of at most 0.0024.
Values may be sent and summed in bfloat16 or wider, within the bound.
A program may use at most 64 MiB of HBM per device.

v0:
```python
import jax
import jax.numpy as jnp
from jax import lax
from jax.sharding import PartitionSpec as P

W = 256
BS = 128
ITERS = 2


regularizer_strength = 0.05
slot_group = 8


def normalize(embed):
    values = embed.astype(jnp.float32)
    factor = lax.rsqrt(jnp.sum(values * values, axis=-1, keepdims=True) + 1e-06)
    return (values * factor).astype(jnp.bfloat16)


def per_device(source_emb, target_emb, source_mass, target_mass, cand_cols, cand_count):
    own_blocks = source_emb.shape[0] // BS
    source_blocks = cand_cols.shape[0]
    slots_each = cand_cols.shape[1]
    target_blocks = own_blocks * lax.axis_size("rows")
    source_unit = normalize(source_emb)
    target_unit = normalize(target_emb)
    source_panel = lax.all_gather(source_unit, "cols", axis=0, tiled=True).reshape(
        source_blocks, BS, W
    )
    live_slot = (jnp.arange(slots_each, dtype=jnp.int32)[None, :] < cand_count).reshape(-1)
    slot_total = source_blocks * slots_each
    padded = -(-slot_total // slot_group) * slot_group
    live_count = live_slot.astype(jnp.int32)
    filled = jnp.sum(live_count)
    placed = jnp.where(
        live_slot, jnp.cumsum(live_count) - 1, filled + jnp.cumsum(1 - live_count) - 1
    )
    slot_source = jnp.repeat(jnp.arange(source_blocks, dtype=jnp.int32), slots_each)
    packed_source = jnp.zeros((padded,), jnp.int32).at[placed].set(slot_source)
    packed_target = jnp.zeros((padded,), jnp.int32).at[placed].set(cand_cols.reshape(-1))
    rounds = (filled + slot_group - 1) // slot_group

    def group_ids(round_index):
        start = round_index * slot_group
        source_ids = lax.dynamic_slice_in_dim(packed_source, start, slot_group)
        target_ids = lax.dynamic_slice_in_dim(packed_target, start, slot_group)
        nonzero_pattern = start + jnp.arange(slot_group, dtype=jnp.int32) < filled
        return (source_ids, target_ids, nonzero_pattern)

    def fresh_kernel(round_index, panel):
        source_ids, target_ids, nonzero_pattern = group_ids(round_index)
        similarity_matrix = jnp.einsum(
            "gaw,gbw->gab",
            source_panel[source_ids],
            panel[target_ids],
            preferred_element_type=jnp.float32,
        )
        return jnp.where(
            nonzero_pattern[:, None, None], jnp.exp(similarity_matrix / regularizer_strength), 0.0
        )

    held_panel = lax.all_gather(target_unit, "rows", axis=0, tiled=True).reshape(
        target_blocks, BS, W
    )

    def kernel_of(round_index):
        return fresh_kernel(round_index, held_panel)

    source_weights = lax.all_gather(source_mass, "cols", axis=0, tiled=True).reshape(
        source_blocks, BS
    )
    target_weights = lax.all_gather(target_mass, "rows", axis=0, tiled=True).reshape(
        target_blocks, BS
    )
    right_dual_multiplier = jnp.ones((target_blocks, BS), jnp.float32)
    for sweep in range(ITERS):

        def row_advance(round_index, totals):
            source_ids, target_ids, nonzero_pattern = group_ids(round_index)
            partial_sums = jnp.einsum(
                "gab,gb->ga",
                kernel_of(round_index),
                right_dual_multiplier[target_ids],
                precision=lax.Precision.HIGHEST,
            )
            return totals.at[source_ids].add(partial_sums)

        row_part = lax.fori_loop(
            0, rounds, row_advance, jnp.zeros((source_blocks, BS), jnp.float32)
        )
        left_dual_multiplier = source_weights / lax.psum(row_part, "cols")

        def col_advance(round_index, totals):
            source_ids, target_ids, nonzero_pattern = group_ids(round_index)
            partial_sums = jnp.einsum(
                "gab,ga->gb",
                kernel_of(round_index),
                left_dual_multiplier[source_ids],
                precision=lax.Precision.HIGHEST,
            )
            return totals.at[target_ids].add(partial_sums)

        col_part = lax.fori_loop(
            0, rounds, col_advance, jnp.zeros((target_blocks, BS), jnp.float32)
        )
        right_dual_multiplier = target_weights / lax.psum(col_part, "rows")
    resident_left_panel = lax.dynamic_slice_in_dim(
        left_dual_multiplier, lax.axis_index("cols") * own_blocks, own_blocks, 0
    )
    resident_right_panel = lax.dynamic_slice_in_dim(
        right_dual_multiplier, lax.axis_index("rows") * own_blocks, own_blocks, 0
    )
    return (
        (regularizer_strength * jnp.log(resident_left_panel)).reshape(-1),
        (regularizer_strength * jnp.log(resident_right_panel)).reshape(-1),
    )


def solution(mesh):
    placed = (
        P(("groups", "rows", "cols"), None),
        P(("groups", "cols", "rows"), None),
        P(("groups", "rows", "cols")),
        P(("groups", "cols", "rows")),
        P(("groups", "rows"), "cols"),
        P(("groups", "rows"), "cols"),
    )
    return jax.shard_map(
        per_device,
        mesh=mesh,
        in_specs=placed,
        out_specs=(P(("groups", "rows", "cols")), P(("groups", "cols", "rows"))),
        check_vma=False,
    )
```

profile of v0, /device:TPU:0, one launch (start us, length us, event | category | flops | bytes accessed | tf_op | source)
XLA Modules:
  0.0 137.9 jit_solution(16340571261952321843)
XLA Ops:
  0.6 0.6 copy-done.5
  1.3 0.7 convert_reduce_fusion
  3.2 0.8 fusion.12
  4.1 0.7 scatter_custom_fusion.4
  4.9 0.7 scatter_custom_fusion.5
  5.9 17.5 %all_gather.13 = bf16[1024,256]{1,0:T(8,128)(2,1)S(1)} all-gather(bf16[256,256]{1,0:T(8,128)(2,1)S(1)} %fusion.9), channel_id=1, replica_groups=mesh['groups'=2,'rows'=4,'cols'=4] {'cols'}, dimensions={0}, use_global_device_ids=true | all-gather | bytes 655360 | tf_op jit(solution)/shard_map/all_gather | solution.py:28
  23.6 7.2 %all_gather.14 = bf16[1024,256]{1,0:T(8,128)(2,1)S(1)} all-gather(bf16[256,256]{1,0:T(8,128)(2,1)S(1)} %fusion.11), channel_id=1, replica_groups=mesh['groups'=2,'rows'=4,'cols'=4] {'rows'}, dimensions={0}, use_global_device_ids=true | all-gather | bytes 655360 | tf_op jit(solution)/shard_map/all_gather | solution.py:63
  30.8 8.8 %while.40 = (s32[]{:T(128)}, f32[8,128]{1,0:T(8,128)S(1)}, s32[]{:T(128)}, s32[32]{0:T(128)S(1)}, s32[]{:T(128)}, /*index=5*/bf16[8,128,256]{2,1,0:T(8,128)(2,1)...) while((s32[]{:T(128)}, f32[8,128]{1,0:T(8,128)S(1)}, ...), condition=%wide.region_9.10_spmd, body=%wide.region_7.9_spmd.sunk | while | flops 68947016 | bytes 4235787 | solution.py:89
  32.1 0.7 add_compare_fusion.8
  33.6 0.9 fusion.66
  34.5 0.6 scatter_fusion
  36.5 0.7 add_compare_fusion.8
  38.0 0.9 fusion.66
  39.6 14.9 %psum.28 = f32[8,128]{1,0:T(8,128)S(1)} all-reduce(f32[8,128]{1,0:T(8,128)S(1)} %get-tuple-element.189), channel_id=1, replica_groups=mesh['groups'=2,'rows'=4,'cols'=4] {'cols'}, use_global_device_ids=true, to_apply=%region_10.11 | all-reduce | flops 1024 | bytes 8192 | tf_op jit(solution)/shard_map/psum | solution.py:92
  54.5 0.7 copy-done.3
  55.2 7.6 %all-gather = f32[4,1,256]{2,1,0:T(1,128)S(1)} all-gather(f32[1,1,256]{2,1,0:T(1,128)S(1)} %bitcast.109), channel_id=1, replica_groups=mesh['groups'=2,'rows'=4,'cols'=4] {'cols'}, dimensions={0}, use_global_device_ids=true | all-gather | bytes 5120 | tf_op jit(solution)/shard_map/all_gather | solution.py:70
  62.7 8.0 %while.41 = (s32[]{:T(128)}, f32[8,128]{1,0:T(8,128)S(1)}, s32[]{:T(128)}, s32[32]{0:T(128)S(1)}, s32[]{:T(128)}, /*index=5*/s32[32]{0:T(128)S(1)}, bf16[8,128,2...) while((s32[]{:T(128)}, f32[8,128]{1,0:T(8,128)S(1)}, ...), condition=%wide.region_13.14_spmd, body=%wide.region_11.13_spmd.sunk | while | flops 68947016 | bytes 4231687 | solution.py:104
  64.0 0.7 add_compare_fusion.9
  68.0 0.7 add_compare_fusion.9
  70.7 12.6 %psum.29 = f32[8,128]{1,0:T(8,128)S(1)} all-reduce(f32[8,128]{1,0:T(8,128)S(1)} %get-tuple-element.190), channel_id=1, replica_groups=mesh['groups'=2,'rows'=4,'cols'=4] {'rows'}, use_global_device_ids=true, to_apply=%region_14.15 | all-reduce | flops 1024 | bytes 8192 | tf_op jit(solution)/shard_map/psum | solution.py:107
  83.4 0.7 copy-done.4
  84.1 5.1 %all-gather.1 = f32[4,1,256]{2,1,0:T(1,128)S(1)} all-gather(f32[1,1,256]{2,1,0:T(1,128)S(1)} %bitcast.110), channel_id=1, replica_groups=mesh['groups'=2,'rows'=4,'cols'=4] {'rows'}, dimensions={0}, use_global_device_ids=true | all-gather | bytes 5120 | tf_op jit(solution)/shard_map/all_gather | solution.py:73
  89.1 8.7 %while.42 = (s32[]{:T(128)}, f32[8,128]{1,0:T(8,128)S(1)}, s32[]{:T(128)}, s32[32]{0:T(128)S(1)}, s32[]{:T(128)}, /*index=5*/bf16[8,128,256]{2,1,0:T(8,128)(2,1)...) while((s32[]{:T(128)}, f32[8,128]{1,0:T(8,128)S(1)}, ...), condition=%wide.region_17.18_spmd, body=%wide.region_15.17_spmd.sunk | while | flops 68947016 | bytes 4231687 | solution.py:89
  90.4 0.7 add_compare_fusion.10
  91.9 0.9 fusion.78
  94.8 0.7 add_compare_fusion.10
  96.3 0.9 fusion.78
  97.9 14.5 %psum.30 = f32[8,128]{1,0:T(8,128)S(1)} all-reduce(f32[8,128]{1,0:T(8,128)S(1)} %get-tuple-element.191), channel_id=1, replica_groups=mesh['groups'=2,'rows'=4,'cols'=4] {'cols'}, use_global_device_ids=true, to_apply=%region_18.19 | all-reduce | flops 1024 | bytes 8192 | tf_op jit(solution)/shard_map/psum | solution.py:92
  112.4 8.0 %while.43 = (s32[]{:T(128)}, f32[8,128]{1,0:T(8,128)S(1)}, s32[]{:T(128)}, s32[32]{0:T(128)S(1)}, s32[]{:T(128)}, /*index=5*/s32[32]{0:T(128)S(1)}, bf16[8,128,2...) while((s32[]{:T(128)}, f32[8,128]{1,0:T(8,128)S(1)}, ...), condition=%wide.region_21.22_spmd, body=%wide.region_19.21_spmd.sunk | while | flops 68947016 | bytes 4231687 | solution.py:104
  113.7 0.7 add_compare_fusion.11
  117.7 0.7 add_compare_fusion.11
  120.4 16.4 %psum.31 = f32[8,128]{1,0:T(8,128)S(1)} all-reduce(f32[8,128]{1,0:T(8,128)S(1)} %get-tuple-element.192), channel_id=1, replica_groups=mesh['groups'=2,'rows'=4,'cols'=4] {'rows'}, use_global_device_ids=true, to_apply=%region_22.23 | all-reduce | flops 1024 | bytes 8192 | tf_op jit(solution)/shard_map/psum | solution.py:107
  (107 shorter events, 25.9 us)
Async XLA Ops:
  0.6 0.7 copy-start.5
  0.6 5.0 %copy-start = (bf16[256,256]{1,0:T(8,128)(2,1)S(1)}, bf16[256,256]{1,0:T(8,128)(2,1)}, u32[]{:S(2)}) copy-start(bf16[256,256]{1,0:T(8,128)(2,1)} %param.14) | copy-start | bytes 393220
  4.0 0.8 copy-start.2
  5.9 17.5 %copy-start.1 = (bf16[256,256]{1,0:T(8,128)(2,1)S(1)}, bf16[256,256]{1,0:T(8,128)(2,1)}, u32[]{:S(2)}) copy-start(bf16[256,256]{1,0:T(8,128)(2,1)} %param.15) | copy-start | bytes 393220
  54.5 0.7 copy-start.3
  83.4 0.7 copy-start.4
where the time goes:
time: 138 us
  blocking collectives  95.7 us (69%)
  local copies, waits for them, and re-layouts  17.7 us (13%)
  other arithmetic  14.2 us (10%)
  matrix products  8.31 us (6%)
  between operations  1.46 us (1%)
    psum x2, blocking collectives, per_device(): left_dual_multiplier = source_weights / lax.psum(row_part, 'cols')  29.4 us
    psum x2, blocking collectives, per_device(): right_dual_multiplier = target_weights / lax.psum(col_part, 'rows')  29 us
    all_gather x1, blocking collectives, per_device(): lax.all_gather(source_unit, 'cols', axis=0, tiled=True)  17.5 us
    all_gather x1, blocking collectives, per_device(): lax.all_gather(source_mass, 'cols', axis=0, tiled=True)  7.56 us
    all_gather x1, blocking collectives, per_device(): lax.all_gather(target_unit, 'rows', axis=0, tiled=True)  7.17 us
    lt x8, other arithmetic, group_ids(): nonzero_pattern = start + jnp.arange(slot_group, dtype=jnp.int32) < filled  5.23 us
    all_gather x1, blocking collectives, per_device(): lax.all_gather(target_mass, 'rows', axis=0, tiled=True)  5.06 us
    gather x8, local copies, waits for them, and re-layouts, fresh_kernel(): source_panel[source_ids]  4.65 us

commit v1 on v0

v1 whole, which is shorter than its diff:
```python
import functools
import math

import jax
import jax.numpy as jnp
from jax import lax
from jax.experimental import pallas as pl
from jax.experimental.pallas import tpu as pltpu
from jax.sharding import PartitionSpec as P

BS = 128
ITERS = 2
strength = 0.05
MESH = pl.DeviceIdType.MESH
NT = (((1,), (1,)), ((), ()))
NN = (((1,), (0,)), ((), ()))


def normalize(embed):
    values = embed.astype(jnp.float32)
    factor = lax.rsqrt(jnp.sum(values * values, axis=-1, keepdims=True) + 1e-06)
    return (values * factor).astype(jnp.bfloat16)


def split_rows(vector):
    high = vector.astype(jnp.bfloat16).astype(jnp.float32)
    row = lax.broadcasted_iota(jnp.int32, (16, vector.shape[1]), 0)
    rows = jnp.where(row == 0, high, jnp.where(row == 1, vector - high, 0.0))
    return rows.astype(jnp.bfloat16)


def kernel(
    n_r, n_c,
    src_ref, tgt_ref, smass_ref, tmass_ref, cand_ref, count_ref,
    spot_ref, tpot_ref,
    sp, tp, sm, tm, mask, gibbs, rbuf, cbuf,
    s_send, s_recv, t_send, t_recv, sm_send, sm_recv, tm_send, tm_recv,
    r_send, r_recv, c_send, c_recv,
):
    me_r, me_c = lax.axis_index("rows"), lax.axis_index("cols")
    m = src_ref.shape[0]
    mb = m // BS
    S, T = n_c * m, n_r * m
    slots = cand_ref.shape[1]

    def to_col(k):
        return lax.rem(me_c + k, n_c)

    def to_row(k):
        return lax.rem(me_r + k, n_r)

    barrier = pltpu.get_barrier_semaphore()
    for k in range(1, n_c):
        pl.semaphore_signal(barrier, inc=1, device_id={"cols": to_col(k)}, device_id_type=MESH)
    for k in range(1, n_r):
        pl.semaphore_signal(barrier, inc=1, device_id={"rows": to_row(k)}, device_id_type=MESH)

    sp[me_c] = normalize(src_ref[...])
    tp[me_r] = normalize(tgt_ref[...])
    sm[me_c] = smass_ref[...]
    tm[me_r] = tmass_ref[...]
    pl.semaphore_wait(barrier, n_c + n_r - 2)

    def col_copy(ref, send, recv, k):
        return pltpu.make_async_remote_copy(
            ref, ref, send, recv, device_id={"cols": to_col(k)}, device_id_type=MESH)

    def row_copy(ref, send, recv, k):
        return pltpu.make_async_remote_copy(
            ref, ref, send, recv, device_id={"rows": to_row(k)}, device_id_type=MESH)

    s_out = [col_copy(sp.at[me_c], s_send.at[k - 1], s_recv.at[k - 1], k) for k in range(1, n_c)]
    t_out = [row_copy(tp.at[me_r], t_send.at[k - 1], t_recv.at[k - 1], k) for k in range(1, n_r)]
    sm_out = [col_copy(sm.at[me_c], sm_send.at[k - 1], sm_recv.at[k - 1], k) for k in range(1, n_c)]
    tm_out = [row_copy(tm.at[me_r], tm_send.at[k - 1], tm_recv.at[k - 1], k) for k in range(1, n_r)]
    for copy in t_out + s_out + sm_out + tm_out:
        copy.start()

    def from_col(ref_of, send, recv, k):
        owner = lax.rem(me_c + n_c - k, n_c)
        col_copy(ref_of(owner), send, recv, k).wait_recv()

    def from_row(ref_of, send, recv, k):
        owner = lax.rem(me_r + n_r - k, n_r)
        row_copy(ref_of(owner), send, recv, k).wait_recv()

    target_block = lax.broadcasted_iota(jnp.int32, mask.shape, 1) // BS
    hit = jnp.zeros(mask.shape, jnp.float32)
    for k in range(slots):
        live = (cand_ref[:, k:k + 1] == target_block) & (count_ref[...] > k)
        hit = jnp.where(live, 1.0, hit)
    mask[...] = hit

    for k in range(1, n_r):
        from_row(lambda o: tp.at[o], t_send.at[k - 1], t_recv.at[k - 1], k)

    ones = jnp.ones((16, T), jnp.bfloat16)
    width = min(T, 1024)
    scale = math.log2(math.e) / strength

    def build(owner):
        for b in range(mb):
            block = sp[owner, b * BS:(b + 1) * BS, :]
            row0 = pl.multiple_of(owner * m + b * BS, BS)
            for t0 in range(0, n_r):
                sim = lax.dot_general(block, tp[t0], NT, preferred_element_type=jnp.float32)
                live = mask[pl.ds(owner * mb + b, 1), t0 * m:(t0 + 1) * m]
                gibbs[pl.ds(row0, BS), t0 * m:(t0 + 1) * m] = (
                    jnp.exp2(sim * scale) * live).astype(jnp.bfloat16)
        rows = pl.ds(pl.multiple_of(owner * m, m), m)
        total = lax.dot_general(ones, gibbs[rows, :], NT, preferred_element_type=jnp.float32)
        rbuf[0, me_c, :, rows] = total[:1]

    build(me_c)
    for k in range(1, n_c):
        from_col(lambda o: sp.at[o], s_send.at[k - 1], s_recv.at[k - 1], k)
        build(lax.rem(me_c + n_c - k, n_c))

    def chunked(extent):
        step = min(extent, 1024)
        return [slice(i, i + step) for i in range(0, extent, step)]

    def exchange_rows(it):
        out = [col_copy(rbuf.at[it, me_c], r_send.at[it, k - 1], r_recv.at[it, k - 1], k)
               for k in range(1, n_c)]
        for copy in out:
            copy.start()
        if it == 0:
            for k in range(1, n_c):
                from_col(lambda o: sm.at[o], sm_send.at[k - 1], sm_recv.at[k - 1], k)
        for k in range(1, n_c):
            from_col(lambda o: rbuf.at[it, o], r_send.at[it, k - 1], r_recv.at[it, k - 1], k)
        total = rbuf[it, 0]
        for j in range(1, n_c):
            total = total + rbuf[it, j]
        return out, jnp.concatenate([sm[j] for j in range(n_c)], axis=1) / total

    def exchange_cols(it):
        out = [row_copy(cbuf.at[it, me_r], c_send.at[it, k - 1], c_recv.at[it, k - 1], k)
               for k in range(1, n_r)]
        for copy in out:
            copy.start()
        if it == 0:
            for k in range(1, n_r):
                from_row(lambda o: tm.at[o], tm_send.at[k - 1], tm_recv.at[k - 1], k)
        for k in range(1, n_r):
            from_row(lambda o: cbuf.at[it, o], c_send.at[it, k - 1], c_recv.at[it, k - 1], k)
        total = cbuf[it, 0]
        for j in range(1, n_r):
            total = total + cbuf[it, j]
        return out, jnp.concatenate([tm[j] for j in range(n_r)], axis=1) / total

    pending = s_out + t_out + sm_out + tm_out
    for it in range(ITERS):
        if it > 0:
            rows = split_rows(v)
            for part in chunked(S):
                total = lax.dot_general(rows, gibbs[part, :], NT, preferred_element_type=jnp.float32)
                rbuf[it, me_c, :, part] = jnp.sum(total, axis=0, keepdims=True)
        out, u = exchange_rows(it)
        pending += out
        rows = split_rows(u)
        for part in chunked(T):
            total = lax.dot_general(rows, gibbs[:, part], NN, preferred_element_type=jnp.float32)
            cbuf[it, me_r, :, part] = jnp.sum(total, axis=0, keepdims=True)
        out, v = exchange_cols(it)
        pending += out

    last = ITERS - 1
    own = pl.ds(pl.multiple_of(me_c * m, m), m)
    total = rbuf[last, 0, :, own]
    for j in range(1, n_c):
        total = total + rbuf[last, j, :, own]
    spot_ref[...] = strength * jnp.log(smass_ref[...] / total)
    own = pl.ds(pl.multiple_of(me_r * m, m), m)
    total = cbuf[last, 0, :, own]
    for j in range(1, n_r):
        total = total + cbuf[last, j, :, own]
    tpot_ref[...] = strength * jnp.log(tmass_ref[...] / total)
    for copy in pending:
        copy.wait_send()


def per_device(source_emb, target_emb, source_mass, target_mass, cand_cols, cand_count):
    n_r, n_c = lax.axis_size("rows"), lax.axis_size("cols")
    m, w = source_emb.shape
    S, T = n_c * m, n_r * m
    vmem = pl.BlockSpec(memory_space=pltpu.VMEM)
    dma = pltpu.SemaphoreType.DMA
    spot, tpot = pl.pallas_call(
        functools.partial(kernel, n_r, n_c),
        out_shape=[jax.ShapeDtypeStruct((1, m), jnp.float32)] * 2,
        in_specs=[vmem] * 6,
        out_specs=[vmem] * 2,
        scratch_shapes=[
            pltpu.VMEM((n_c, m, w), jnp.bfloat16),
            pltpu.VMEM((n_r, m, w), jnp.bfloat16),
            pltpu.VMEM((n_c, 1, m), jnp.float32),
            pltpu.VMEM((n_r, 1, m), jnp.float32),
            pltpu.VMEM((cand_cols.shape[0], T), jnp.float32),
            pltpu.VMEM((S, T), jnp.bfloat16),
            pltpu.VMEM((ITERS, n_c, 1, S), jnp.float32),
            pltpu.VMEM((ITERS, n_r, 1, T), jnp.float32),
            dma((n_c - 1,)), dma((n_c - 1,)), dma((n_r - 1,)), dma((n_r - 1,)),
            dma((n_c - 1,)), dma((n_c - 1,)), dma((n_r - 1,)), dma((n_r - 1,)),
            dma((ITERS, n_c - 1)), dma((ITERS, n_c - 1)),
            dma((ITERS, n_r - 1)), dma((ITERS, n_r - 1)),
        ],
        compiler_params=pltpu.CompilerParams(
            collective_id=0, has_side_effects=True,
            vmem_limit_bytes=min(58 << 20, 2 * S * T + (24 << 20)),
        ),
        name="sinkhorn",
    )(source_emb, target_emb, source_mass.reshape(1, m), target_mass.reshape(1, m),
      cand_cols, cand_count)
    return spot.reshape(-1), tpot.reshape(-1)


def solution(mesh):
    placed = (
        P(("groups", "rows", "cols"), None),
        P(("groups", "cols", "rows"), None),
        P(("groups", "rows", "cols")),
        P(("groups", "cols", "rows")),
        P(("groups", "rows"), "cols"),
        P(("groups", "rows"), "cols"),
    )
    return jax.shard_map(
        per_device,
        mesh=mesh,
        in_specs=placed,
        out_specs=(P(("groups", "rows", "cols")), P(("groups", "cols", "rows"))),
        check_vma=False,
    )
```

time: 138 us -> 38.3 us (0.28)
  blocking collectives: 95.7 us -> 0 us
  Pallas kernels: 0 us -> 32.4 us
  other arithmetic: 14.2 us -> 0 us
  local copies, waits for them, and re-layouts: 17.7 us -> 4.96 us
  matrix products: 8.31 us -> 0 us
    psum x4 -> x0, blocking collectives: 58.4 us -> none  [the longest x2 29.4 us: per_device(): left_dual_multiplier = source_weights / lax.psum(row_part, 'cols')]
    all_gather x4 -> x0, blocking collectives: 37.3 us -> none  [the longest x1 17.5 us: per_device(): lax.all_gather(source_unit, 'cols', axis=0, tiled=True)]
    pallas_call x0 -> x1, Pallas kernels: none -> 32.4 us  [per_device(): pl.pallas_call(functools.partial(kernel, n_r, n_c), out_shape=[jax.ShapeD...]
    gather x24 -> x0, local copies, waits for them, and re-layouts: 13.7 us -> none  [the longest x8 4.65 us: fresh_kernel(): source_panel[source_ids]]
    dot_general x16 -> x0, matrix products: 8.31 us -> none  [the longest x4 3.66 us: row_advance(): jnp.einsum('gab,gb->ga', kernel_of(round_index), right_dual_multiplier[ta...]
    lt x9 -> x0, other arithmetic: 5.3 us -> none  [the longest x8 5.23 us: group_ids(): nonzero_pattern = start + jnp.arange(slot_group, dtype=jnp.int32) < filled]
    scatter-add x8 -> x0, other arithmetic: 4.96 us -> none  [the longest x4 2.5 us: row_advance(): return totals.at[source_ids].add(partial_sums)]
    unnamed x13 -> x16, local copies, waits for them, and re-layouts: 2.09 us -> 4.96 us
where the time goes in v1:
time: 38.3 us; the launch traced here: 38 us
  Pallas kernels  32.4 us (85%)
  local copies, waits for them, and re-layouts  4.96 us (13%)
  between operations  0.65 us (2%)
    pallas_call x1, Pallas kernels, per_device(): pl.pallas_call(functools.partial(kernel, n_r, n_c), out_shape=[jax.ShapeD...  32.4 us
    unnamed x16, local copies, waits for them, and re-layouts  4.96 us

profile of v1, /device:TPU:0, one launch (start us, length us, event | category | flops | bytes accessed | tf_op | source)
XLA Modules:
  0.0 38.0 jit_solution(5275160213831966198)
XLA Ops:
  0.6 0.0 copy-start.4
  0.6 0.7 %copy-done.4 = s32[8,4]{0,1:T(4,128)S(1)} copy-done((s32[8,4]{0,1:T(4,128)S(1)}, s32[8,4]{0,1:T(4,128)}, u32[]{:S(2)}) %copy-start.4) | copy-done | bytes 152
  1.3 0.0 copy-start.5
  1.3 0.1 copy.8.cand_ref
  1.4 0.6 %copy-done.5 = s32[8,1]{0,1:T(1,128)S(1)} copy-done((s32[8,1]{0,1:T(1,128)S(1)}, s32[8,1]{0,1:T(1,128)}, u32[]{:S(2)}) %copy-start.5) | copy-done | bytes 56
  2.0 0.0 copy-start.2
  2.0 0.0 copy-start.3
  2.0 0.1 copy.9.count_ref
  2.1 0.6 %copy-done.2 = f32[256]{0:T(256)S(1)} copy-done((f32[256]{0:T(256)S(1)}, f32[256]{0:T(256)}, u32[]{:S(2)}) %copy-start.2) | copy-done | bytes 1048
  2.6 0.0 copy-done.3
  2.7 0.0 copy-start
  2.7 0.9 %copy-done = bf16[256,256]{1,0:T(8,128)(2,1)S(1)} copy-done((bf16[256,256]{1,0:T(8,128)(2,1)S(1)}, bf16[256,256]{1,0:T(8,128)(2,1)}, u32[]{:S(2)}) %copy-start) | copy-done | bytes 131096
  3.6 0.0 copy-start.1
  3.6 0.9 %copy-done.1 = bf16[256,256]{1,0:T(8,128)(2,1)S(1)} copy-done((bf16[256,256]{1,0:T(8,128)(2,1)S(1)}, bf16[256,256]{1,0:T(8,128)(2,1)}, u32[]{:S(2)}) %copy-start.1) | copy-done | bytes 131096
  4.5 32.4 %sinkhorn.1 = (f32[1,256]{1,0:T(1,128)S(1)}, f32[1,256]{1,0:T(1,128)S(1)}) custom-call(bf16[256,256]{1,0:T(8,128)(2,1)S(1)} %copy-done, bf16[256,256]{1,0:T(8,128)(2,1)S(1)} %copy-done.1, f32[1,256]{1,0:T(1,128)S(1)} %bitcast.4, f32[1,256]{1,0:T(1,128)S(1)} %bitcast.5, s32[8,4]{1,0:T(8,128)S(1)} %copy.8.cand_ref, s32[8,1]{1,0:T(8,128)S(1)} %copy.9.count_ref), custom_call_target="tpu_custom_call" | custom-call | tf_op jit(solution)/shard_map/sinkhorn/pallas_call | solution.py:190
  36.9 0.6 %copy.12 = f32[256]{0:T(256)} copy(f32[256]{0:T(256)S(1)} %bitcast.7) | data formatting | bytes 2048
  37.5 0.6 %copy.13 = f32[256]{0:T(256)} copy(f32[256]{0:T(256)S(1)} %bitcast.6) | data formatting | bytes 2048
Async XLA Ops:
  0.6 0.7 %copy-start.4 = (s32[8,4]{0,1:T(4,128)S(1)}, s32[8,4]{0,1:T(4,128)}, u32[]{:S(2)}) copy-start(s32[8,4]{0,1:T(4,128)} %param.10) | copy-start | bytes 388
  1.3 0.7 %copy-start.5 = (s32[8,1]{0,1:T(1,128)S(1)}, s32[8,1]{0,1:T(1,128)}, u32[]{:S(2)}) copy-start(s32[8,1]{0,1:T(1,128)} %param.11) | copy-start | bytes 100
  2.0 0.7 %copy-start.2 = (f32[256]{0:T(256)S(1)}, f32[256]{0:T(256)}, u32[]{:S(2)}) copy-start(f32[256]{0:T(256)} %param.8) | copy-start | bytes 3076
  2.0 0.7 %copy-start.3 = (f32[256]{0:T(256)S(1)}, f32[256]{0:T(256)}, u32[]{:S(2)}) copy-start(f32[256]{0:T(256)} %param.9) | copy-start | bytes 3076
  2.7 0.9 %copy-start = (bf16[256,256]{1,0:T(8,128)(2,1)S(1)}, bf16[256,256]{1,0:T(8,128)(2,1)}, u32[]{:S(2)}) copy-start(bf16[256,256]{1,0:T(8,128)(2,1)} %src_ref.1) | copy-start | bytes 393220
  3.6 0.9 %copy-start.1 = (bf16[256,256]{1,0:T(8,128)(2,1)S(1)}, bf16[256,256]{1,0:T(8,128)(2,1)}, u32[]{:S(2)}) copy-start(bf16[256,256]{1,0:T(8,128)(2,1)} %tgt_ref.1) | copy-start | bytes 393220

commit v2 on v1

--- a/solution.py
+++ b/solution.py
@@ -31,9 +31,9 @@
 
 def kernel(
     n_r, n_c,
-    src_ref, tgt_ref, smass_ref, tmass_ref, cand_ref, count_ref,
-    spot_ref, tpot_ref,
-    sp, tp, sm, tm, mask, gibbs, rbuf, cbuf,
+    src_hbm, tgt_hbm, smass_hbm, tmass_hbm, cand_hbm, count_hbm,
+    pot_ref,
+    src_ref, tgt_ref, cand_ref, count_ref, in_sem, sp, tp, sm, tm, mask, gibbs, rbuf, cbuf,
     s_send, s_recv, t_send, t_recv, sm_send, sm_recv, tm_send, tm_recv,
     r_send, r_recv, c_send, c_recv,
 ):
@@ -41,13 +41,23 @@
     m = src_ref.shape[0]
     mb = m // BS
     S, T = n_c * m, n_r * m
-    slots = cand_ref.shape[1]
+    slots, blocks = cand_ref.shape
+    relayed = n_c == 4
 
     def to_col(k):
         return lax.rem(me_c + k, n_c)
 
     def to_row(k):
         return lax.rem(me_r + k, n_r)
+
+    sm_own, tm_own = sm.at[me_c], tm.at[me_r]
+    loads = [
+        pltpu.make_async_copy(a, b, in_sem.at[i]) for i, (a, b) in enumerate((
+            (src_hbm, src_ref), (tgt_hbm, tgt_ref), (smass_hbm, sm_own),
+            (tmass_hbm, tm_own), (cand_hbm, cand_ref), (count_hbm, count_ref)))
+    ]
+    for load in loads:
+        load.start()
 
     barrier = pltpu.get_barrier_semaphore()
     for k in range(1, n_c):
@@ -55,10 +65,12 @@
     for k in range(1, n_r):
         pl.semaphore_signal(barrier, inc=1, device_id={"rows": to_row(k)}, device_id_type=MESH)
 
+    loads[0].wait()
     sp[me_c] = normalize(src_ref[...])
+    loads[1].wait()
     tp[me_r] = normalize(tgt_ref[...])
-    sm[me_c] = smass_ref[...]
-    tm[me_r] = tmass_ref[...]
+    for load in loads[2:]:
+        load.wait()
     pl.semaphore_wait(barrier, n_c + n_r - 2)
 
     def col_copy(ref, send, recv, k):
@@ -69,11 +81,37 @@
         return pltpu.make_async_remote_copy(
             ref, ref, send, recv, device_id={"rows": to_row(k)}, device_id_type=MESH)
 
-    s_out = [col_copy(sp.at[me_c], s_send.at[k - 1], s_recv.at[k - 1], k) for k in range(1, n_c)]
+    def piece(owner, h):
+        return sp.at[owner, pl.ds(h * BS, BS)]
+
+    def s_copy(owner, target, k, h):
+        return pltpu.make_async_remote_copy(
+            piece(owner, h), piece(owner, h), s_send.at[k - 1, h], s_recv.at[k - 1, h],
+            device_id={"cols": target}, device_id_type=MESH)
+
+    def s_arrive(owner, h):
+        s_copy(owner, to_col(1), lax.rem(me_c + n_c - owner, n_c), h).wait_recv()
+
+    inner = (me_c == 1) | (me_c == 2)
+    if relayed:
+        near = jnp.where(me_c >= 2, 3, 1)
+        for k in (near, 4 - near):
+            for h in range(mb):
+                s_copy(me_c, to_col(k), k, h).start()
+
+        @pl.when(jnp.logical_not(inner))
+        def _():
+            for h in range(mb):
+                s_copy(me_c, to_col(2), 2, h).start()
+    else:
+        for k in range(1, n_c):
+            for h in range(mb):
+                s_copy(me_c, to_col(k), k, h).start()
+
     t_out = [row_copy(tp.at[me_r], t_send.at[k - 1], t_recv.at[k - 1], k) for k in range(1, n_r)]
     sm_out = [col_copy(sm.at[me_c], sm_send.at[k - 1], sm_recv.at[k - 1], k) for k in range(1, n_c)]
     tm_out = [row_copy(tm.at[me_r], tm_send.at[k - 1], tm_recv.at[k - 1], k) for k in range(1, n_r)]
-    for copy in t_out + s_out + sm_out + tm_out:
+    for copy in t_out + sm_out + tm_out:
         copy.start()
 
     def from_col(ref_of, send, recv, k):
@@ -86,10 +124,27 @@
 
     target_block = lax.broadcasted_iota(jnp.int32, mask.shape, 1) // BS
     hit = jnp.zeros(mask.shape, jnp.float32)
+    diagonal = (lax.broadcasted_iota(jnp.int32, (blocks, blocks), 0)
+                == lax.broadcasted_iota(jnp.int32, (blocks, blocks), 1))
+
+    def as_column(row):
+        return jnp.sum(jnp.where(diagonal, row.astype(jnp.float32), 0.0), axis=1, keepdims=True)
+
+    counts = as_column(count_ref[...])
     for k in range(slots):
-        live = (cand_ref[:, k:k + 1] == target_block) & (count_ref[...] > k)
+        named = as_column(cand_ref[k:k + 1, :]).astype(jnp.int32)
+        live = (named == target_block) & (counts > k)
         hit = jnp.where(live, 1.0, hit)
     mask[...] = hit
+
+    first = 1 + lax.rem(me_c, 2)
+    if relayed:
+        for h in range(mb):
+            s_arrive(first, h)
+
+            @pl.when(inner)
+            def _():
+                s_copy(first, 3 * me_c - 3, 2, h).start()
 
     for k in range(1, n_r):
         from_row(lambda o: tp.at[o], t_send.at[k - 1], t_recv.at[k - 1], k)
@@ -98,8 +153,10 @@
     width = min(T, 1024)
     scale = math.log2(math.e) / strength
 
-    def build(owner):
+    def build(owner, awaited=True):
         for b in range(mb):
+            if awaited:
+                s_arrive(owner, b)
             block = sp[owner, b * BS:(b + 1) * BS, :]
             row0 = pl.multiple_of(owner * m + b * BS, BS)
             for t0 in range(0, n_r):
@@ -111,10 +168,17 @@
         total = lax.dot_general(ones, gibbs[rows, :], NT, preferred_element_type=jnp.float32)
         rbuf[0, me_c, :, rows] = total[:1]
 
-    build(me_c)
-    for k in range(1, n_c):
-        from_col(lambda o: sp.at[o], s_send.at[k - 1], s_recv.at[k - 1], k)
-        build(lax.rem(me_c + n_c - k, n_c))
+    build(me_c, awaited=False)
+    if relayed:
+        build(first, awaited=False)
+        build(3 * lax.rem(me_c + 1, 2))
+        build(to_col(2))
+    else:
+        def arrive(k, carry):
+            build(to_col(k))
+            return carry
+
+        lax.fori_loop(1, n_c, arrive, 0)
 
     def chunked(extent):
         step = min(extent, 1024)
@@ -150,7 +214,7 @@
             total = total + cbuf[it, j]
         return out, jnp.concatenate([tm[j] for j in range(n_r)], axis=1) / total
 
-    pending = s_out + t_out + sm_out + tm_out
+    pending = t_out + sm_out + tm_out
     for it in range(ITERS):
         if it > 0:
             rows = split_rows(v)
@@ -171,14 +235,17 @@
     total = rbuf[last, 0, :, own]
     for j in range(1, n_c):
         total = total + rbuf[last, j, :, own]
-    spot_ref[...] = strength * jnp.log(smass_ref[...] / total)
+    pot_ref[0:1] = strength * jnp.log(sm[me_c] / total)
     own = pl.ds(pl.multiple_of(me_r * m, m), m)
     total = cbuf[last, 0, :, own]
     for j in range(1, n_r):
         total = total + cbuf[last, j, :, own]
-    tpot_ref[...] = strength * jnp.log(tmass_ref[...] / total)
+    pot_ref[1:2] = strength * jnp.log(tm[me_r] / total)
     for copy in pending:
         copy.wait_send()
+    for k in range(1, n_c):
+        for h in range(mb):
+            s_copy(me_c, to_col(k), k, h).wait_send()
 
 
 def per_device(source_emb, target_emb, source_mass, target_mass, cand_cols, cand_count):
@@ -187,33 +254,40 @@
     S, T = n_c * m, n_r * m
     vmem = pl.BlockSpec(memory_space=pltpu.VMEM)
     dma = pltpu.SemaphoreType.DMA
-    spot, tpot = pl.pallas_call(
+    slots, blocks = cand_cols.shape[1], cand_cols.shape[0]
+    pots = pl.pallas_call(
         functools.partial(kernel, n_r, n_c),
-        out_shape=[jax.ShapeDtypeStruct((1, m), jnp.float32)] * 2,
-        in_specs=[vmem] * 6,
-        out_specs=[vmem] * 2,
+        out_shape=jax.ShapeDtypeStruct((2, m), jnp.float32),
+        in_specs=[pl.BlockSpec(memory_space=pltpu.HBM)] * 6,
+        out_specs=vmem,
         scratch_shapes=[
+            pltpu.VMEM((m, w), jnp.bfloat16),
+            pltpu.VMEM((m, w), jnp.bfloat16),
+            pltpu.VMEM((slots, blocks), jnp.int32),
+            pltpu.VMEM((1, blocks), jnp.int32),
+            dma((6,)),
             pltpu.VMEM((n_c, m, w), jnp.bfloat16),
             pltpu.VMEM((n_r, m, w), jnp.bfloat16),
             pltpu.VMEM((n_c, 1, m), jnp.float32),
             pltpu.VMEM((n_r, 1, m), jnp.float32),
-            pltpu.VMEM((cand_cols.shape[0], T), jnp.float32),
+            pltpu.VMEM((blocks, T), jnp.float32),
             pltpu.VMEM((S, T), jnp.bfloat16),
             pltpu.VMEM((ITERS, n_c, 1, S), jnp.float32),
             pltpu.VMEM((ITERS, n_r, 1, T), jnp.float32),
-            dma((n_c - 1,)), dma((n_c - 1,)), dma((n_r - 1,)), dma((n_r - 1,)),
+            dma((n_c - 1, m // BS)), dma((n_c - 1, m // BS)),
+            dma((n_r - 1,)), dma((n_r - 1,)),
             dma((n_c - 1,)), dma((n_c - 1,)), dma((n_r - 1,)), dma((n_r - 1,)),
             dma((ITERS, n_c - 1)), dma((ITERS, n_c - 1)),
             dma((ITERS, n_r - 1)), dma((ITERS, n_r - 1)),
         ],
         compiler_params=pltpu.CompilerParams(
             collective_id=0, has_side_effects=True,
-            vmem_limit_bytes=min(58 << 20, 2 * S * T + (24 << 20)),
+            vmem_limit_bytes=63 << 20,
         ),
         name="sinkhorn",
     )(source_emb, target_emb, source_mass.reshape(1, m), target_mass.reshape(1, m),
-      cand_cols, cand_count)
-    return spot.reshape(-1), tpot.reshape(-1)
+      cand_cols.T, cand_count.T)
+    return pots[0], pots[1]
 
 
 def solution(mesh):

time: 38.3 us -> 33 us (0.86)
  local copies, waits for them, and re-layouts: 4.96 us -> 1.32 us
  Pallas kernels: 32.4 us -> 30.8 us
    unnamed x16 -> x0, local copies, waits for them, and re-layouts: 4.96 us -> none
    pallas_call x1, Pallas kernels: 32.4 us -> 30.8 us  [per_device(): pl.pallas_call(functools.partial(kernel, n_r, n_c), out_shape=jax.ShapeDt...]
    slice x0 -> x1, local copies, waits for them, and re-layouts: none -> 1.32 us  [per_device(): return (pots[0], pots[1])]
where the time goes in v2:
time: 33 us; the launch traced here: 32.8 us
  Pallas kernels  30.8 us (93%)
  local copies, waits for them, and re-layouts  1.32 us (4%)
  between operations  0.64 us (2%)
    pallas_call x1, Pallas kernels, per_device(): pl.pallas_call(functools.partial(kernel, n_r, n_c), out_shape=jax.ShapeDt...  30.8 us
    slice x1, local copies, waits for them, and re-layouts, per_device(): return (pots[0], pots[1])  1.32 us

profile of v2, /device:TPU:0, one launch (start us, length us, event | category | flops | bytes accessed | tf_op | source)
XLA Modules:
  0.0 32.8 jit_solution(18337523408673258107)
XLA Ops:
  0.6 30.8 %sinkhorn.1 = f32[2,256]{1,0:T(2,128)} custom-call(bf16[256,256]{1,0:T(8,128)(2,1)} %src_hbm.1, bf16[256,256]{1,0:T(8,128)(2,1)} %tgt_hbm.1, f32[1,256]{1,0:T(1,128)} %bitcast.7, f32[1,256]{1,0:T(1,128)} %bitcast.8, s32[4,8]{1,0:T(4,128)} %bitcast.6, s32[1,8]{1,0:T(1,128)} %bitcast.11), custom_call_target="tpu_custom_call" | custom-call | tf_op jit(solution)/shard_map/sinkhorn/pallas_call | solution.py:258
  31.5 1.3 %fusion = (f32[1,256]{1,0:T(1,128)}, f32[1,256]{1,0:T(1,128)}) fusion(f32[2,256]{1,0:T(2,128)} %sinkhorn.1), kind=kLoop, calls=%fused_computation | loop fusion | bytes 4096 | tf_op jit(solution)/shard_map/slice | solution.py:290

commit v3 on v2

--- a/solution.py
+++ b/solution.py
@@ -33,7 +33,7 @@
     n_r, n_c,
     src_hbm, tgt_hbm, smass_hbm, tmass_hbm, cand_hbm, count_hbm,
     pot_ref,
-    src_ref, tgt_ref, cand_ref, count_ref, in_sem, sp, tp, sm, tm, mask, gibbs, rbuf, cbuf,
+    src_ref, tgt_ref, smine, cand_own, count_own, cand_ref, count_ref, pout, pin, in_sem, swap_send, swap_recv, sp, tp, sm, tm, mask, gibbs, rbuf, cbuf,
     s_send, s_recv, t_send, t_recv, sm_send, sm_recv, tm_send, tm_recv,
     r_send, r_recv, c_send, c_recv,
 ):
@@ -43,6 +43,16 @@
     S, T = n_c * m, n_r * m
     slots, blocks = cand_ref.shape
     relayed = n_c == 4
+    odd = lax.rem(me_c, 2)
+
+    def flip(row, bit):
+        return row + bit * (1 - 2 * lax.rem(row, 2))
+
+    role = flip(me_r, odd)
+
+    def holder(row, col):
+        return {"rows": flip(row, lax.rem(col, 2)), "cols": col}
+
 
     def to_col(k):
         return lax.rem(me_c + k, n_c)
@@ -50,32 +60,44 @@
     def to_row(k):
         return lax.rem(me_r + k, n_r)
 
-    sm_own, tm_own = sm.at[me_c], tm.at[me_r]
+    tm_own = tm.at[me_r]
     loads = [
         pltpu.make_async_copy(a, b, in_sem.at[i]) for i, (a, b) in enumerate((
-            (src_hbm, src_ref), (tgt_hbm, tgt_ref), (smass_hbm, sm_own),
-            (tmass_hbm, tm_own), (cand_hbm, cand_ref), (count_hbm, count_ref)))
+            (src_hbm, src_ref), (tgt_hbm, tgt_ref), (smass_hbm, smine),
+            (tmass_hbm, tm_own), (cand_hbm, cand_own), (count_hbm, count_own)))
     ]
     for load in loads:
         load.start()
 
     barrier = pltpu.get_barrier_semaphore()
     for k in range(1, n_c):
-        pl.semaphore_signal(barrier, inc=1, device_id={"cols": to_col(k)}, device_id_type=MESH)
+        for row in (me_r, flip(me_r, 1)):
+            pl.semaphore_signal(
+                barrier, inc=1, device_id={"rows": row, "cols": to_col(k)}, device_id_type=MESH)
     for k in range(1, n_r):
         pl.semaphore_signal(barrier, inc=1, device_id={"rows": to_row(k)}, device_id_type=MESH)
 
     loads[0].wait()
-    sp[me_c] = normalize(src_ref[...])
+    src_ref[...] = normalize(src_ref[...])
     loads[1].wait()
     tp[me_r] = normalize(tgt_ref[...])
     for load in loads[2:]:
         load.wait()
-    pl.semaphore_wait(barrier, n_c + n_r - 2)
-
-    def col_copy(ref, send, recv, k):
+    pl.semaphore_wait(barrier, 2 * (n_c - 1) + n_r - 1)
+
+    def col_copy(src, dst, send, recv, k, row):
         return pltpu.make_async_remote_copy(
-            ref, ref, send, recv, device_id={"cols": to_col(k)}, device_id_type=MESH)
+            src, dst, send, recv, device_id=holder(row, to_col(k)), device_id_type=MESH)
+
+    def swap(i, src, dst):
+        return pltpu.make_async_remote_copy(
+            src, dst, swap_send.at[i], swap_recv.at[i],
+            device_id={"rows": flip(me_r, 1)}, device_id_type=MESH)
+
+    swaps = [
+        swap(0, src_ref, sp.at[me_c]), swap(1, smine, sm.at[me_c]),
+        swap(2, cand_own, cand_ref), swap(3, count_own, count_ref),
+    ]
 
     def row_copy(ref, send, recv, k):
         return pltpu.make_async_remote_copy(
@@ -84,10 +106,15 @@
     def piece(owner, h):
         return sp.at[owner, pl.ds(h * BS, BS)]
 
-    def s_copy(owner, target, k, h):
+    def s_copy(owner, target, k, h, src=None):
+        row = me_r if src is not None else role
         return pltpu.make_async_remote_copy(
-            piece(owner, h), piece(owner, h), s_send.at[k - 1, h], s_recv.at[k - 1, h],
-            device_id={"cols": target}, device_id_type=MESH)
+            piece(owner, h) if src is None else src, piece(owner, h),
+            s_send.at[k - 1, h], s_recv.at[k - 1, h],
+            device_id=holder(row, target), device_id_type=MESH)
+
+    def own_copy(k, h):
+        return s_copy(me_c, to_col(k), k, h, src_ref.at[pl.ds(h * BS, BS)])
 
     def s_arrive(owner, h):
         s_copy(owner, to_col(1), lax.rem(me_c + n_c - owner, n_c), h).wait_recv()
@@ -97,30 +124,48 @@
         near = jnp.where(me_c >= 2, 3, 1)
         for k in (near, 4 - near):
             for h in range(mb):
-                s_copy(me_c, to_col(k), k, h).start()
+                own_copy(k, h).start()
 
         @pl.when(jnp.logical_not(inner))
         def _():
             for h in range(mb):
-                s_copy(me_c, to_col(2), 2, h).start()
+                own_copy(2, h).start()
     else:
         for k in range(1, n_c):
             for h in range(mb):
-                s_copy(me_c, to_col(k), k, h).start()
+                own_copy(k, h).start()
+
+    @pl.when(odd == 1)
+    def _():
+        for copy in swaps:
+            copy.start()
+
+    @pl.when(odd == 0)
+    def _():
+        sp[me_c] = src_ref[...]
+        sm[me_c] = smine[...]
+        cand_ref[...] = cand_own[...]
+        count_ref[...] = count_own[...]
 
     t_out = [row_copy(tp.at[me_r], t_send.at[k - 1], t_recv.at[k - 1], k) for k in range(1, n_r)]
-    sm_out = [col_copy(sm.at[me_c], sm_send.at[k - 1], sm_recv.at[k - 1], k) for k in range(1, n_c)]
+    sm_out = [col_copy(smine, sm.at[me_c], sm_send.at[k - 1], sm_recv.at[k - 1], k, me_r)
+              for k in range(1, n_c)]
     tm_out = [row_copy(tm.at[me_r], tm_send.at[k - 1], tm_recv.at[k - 1], k) for k in range(1, n_r)]
     for copy in t_out + sm_out + tm_out:
         copy.start()
 
     def from_col(ref_of, send, recv, k):
         owner = lax.rem(me_c + n_c - k, n_c)
-        col_copy(ref_of(owner), send, recv, k).wait_recv()
+        col_copy(ref_of(owner), ref_of(owner), send, recv, k, role).wait_recv()
 
     def from_row(ref_of, send, recv, k):
         owner = lax.rem(me_r + n_r - k, n_r)
         row_copy(ref_of(owner), send, recv, k).wait_recv()
+
+    @pl.when(odd == 1)
+    def _():
+        for copy in swaps:
+            copy.wait_recv()
 
     target_block = lax.broadcasted_iota(jnp.int32, mask.shape, 1) // BS
     hit = jnp.zeros(mask.shape, jnp.float32)
@@ -185,7 +230,8 @@
         return [slice(i, i + step) for i in range(0, extent, step)]
 
     def exchange_rows(it):
-        out = [col_copy(rbuf.at[it, me_c], r_send.at[it, k - 1], r_recv.at[it, k - 1], k)
+        out = [col_copy(rbuf.at[it, me_c], rbuf.at[it, me_c],
+                        r_send.at[it, k - 1], r_recv.at[it, k - 1], k, role)
                for k in range(1, n_c)]
         for copy in out:
             copy.start()
@@ -199,11 +245,44 @@
             total = total + rbuf[it, j]
         return out, jnp.concatenate([sm[j] for j in range(n_c)], axis=1) / total
 
+    pending = t_out + sm_out + tm_out
+    home = swap(4, pout, pin)
+
+    def source_side():
+        own = pl.ds(pl.multiple_of(me_c * m, m), m)
+        total = rbuf[ITERS - 1, 0, :, own]
+        for j in range(1, n_c):
+            total = total + rbuf[ITERS - 1, j, :, own]
+        pout[...] = strength * jnp.log(sm[me_c] / total)
+
+        @pl.when(odd == 1)
+        def _():
+            home.start()
+            for copy in swaps:
+                copy.wait_send()
+
+        for copy in pending:
+            copy.wait_send()
+        for k in range(1, n_c):
+            for h in range(mb):
+                own_copy(k, h).wait_send()
+
+        @pl.when(odd == 1)
+        def _():
+            home.wait()
+            pot_ref[0:1] = pin[...]
+
+        @pl.when(odd == 0)
+        def _():
+            pot_ref[0:1] = pout[...]
+
     def exchange_cols(it):
         out = [row_copy(cbuf.at[it, me_r], c_send.at[it, k - 1], c_recv.at[it, k - 1], k)
                for k in range(1, n_r)]
         for copy in out:
             copy.start()
+        if it == ITERS - 1:
+            source_side()
         if it == 0:
             for k in range(1, n_r):
                 from_row(lambda o: tm.at[o], tm_send.at[k - 1], tm_recv.at[k - 1], k)
@@ -214,7 +293,6 @@
             total = total + cbuf[it, j]
         return out, jnp.concatenate([tm[j] for j in range(n_r)], axis=1) / total
 
-    pending = t_out + sm_out + tm_out
     for it in range(ITERS):
         if it > 0:
             rows = split_rows(v)
@@ -228,24 +306,17 @@
             total = lax.dot_general(rows, gibbs[:, part], NN, preferred_element_type=jnp.float32)
             cbuf[it, me_r, :, part] = jnp.sum(total, axis=0, keepdims=True)
         out, v = exchange_cols(it)
-        pending += out
+        if it < ITERS - 1:
+            pending += out
 
     last = ITERS - 1
-    own = pl.ds(pl.multiple_of(me_c * m, m), m)
-    total = rbuf[last, 0, :, own]
-    for j in range(1, n_c):
-        total = total + rbuf[last, j, :, own]
-    pot_ref[0:1] = strength * jnp.log(sm[me_c] / total)
     own = pl.ds(pl.multiple_of(me_r * m, m), m)
     total = cbuf[last, 0, :, own]
     for j in range(1, n_r):
         total = total + cbuf[last, j, :, own]
     pot_ref[1:2] = strength * jnp.log(tm[me_r] / total)
-    for copy in pending:
+    for copy in out:
         copy.wait_send()
-    for k in range(1, n_c):
-        for h in range(mb):
-            s_copy(me_c, to_col(k), k, h).wait_send()
 
 
 def per_device(source_emb, target_emb, source_mass, target_mass, cand_cols, cand_count):
@@ -263,9 +334,14 @@
         scratch_shapes=[
             pltpu.VMEM((m, w), jnp.bfloat16),
             pltpu.VMEM((m, w), jnp.bfloat16),
+            pltpu.VMEM((1, m), jnp.float32),
             pltpu.VMEM((slots, blocks), jnp.int32),
             pltpu.VMEM((1, blocks), jnp.int32),
-            dma((6,)),
+            pltpu.VMEM((slots, blocks), jnp.int32),
+            pltpu.VMEM((1, blocks), jnp.int32),
+            pltpu.VMEM((1, m), jnp.float32),
+            pltpu.VMEM((1, m), jnp.float32),
+            dma((6,)), dma((5,)), dma((5,)),
             pltpu.VMEM((n_c, m, w), jnp.bfloat16),
             pltpu.VMEM((n_r, m, w), jnp.bfloat16),
             pltpu.VMEM((n_c, 1, m), jnp.float32),

time: 33 us -> 32.7 us (level)
  no operation moved by 1% of the time
where the time goes in v3:
time: 32.7 us; the launch traced here: 32.5 us
  Pallas kernels  30.6 us (94%)
  local copies, waits for them, and re-layouts  1.32 us (4%)
  between operations  0.64 us (2%)
    pallas_call x1, Pallas kernels, per_device(): pl.pallas_call(functools.partial(kernel, n_r, n_c), out_shape=jax.ShapeDt...  30.6 us
    slice x1, local copies, waits for them, and re-layouts, per_device(): return (pots[0], pots[1])  1.32 us

profile of v3, /device:TPU:0, one launch (start us, length us, event | category | flops | bytes accessed | tf_op | source)
XLA Modules:
  0.0 32.5 jit_solution(13653192757411288626)
XLA Ops:
  0.6 30.6 %sinkhorn.1 = f32[2,256]{1,0:T(2,128)} custom-call(bf16[256,256]{1,0:T(8,128)(2,1)} %src_hbm.1, bf16[256,256]{1,0:T(8,128)(2,1)} %tgt_hbm.1, f32[1,256]{1,0:T(1,128)} %bitcast.7, f32[1,256]{1,0:T(1,128)} %bitcast.8, s32[4,8]{1,0:T(4,128)} %bitcast.6, s32[1,8]{1,0:T(1,128)} %bitcast.11), custom_call_target="tpu_custom_call" | custom-call | tf_op jit(solution)/shard_map/sinkhorn/pallas_call | solution.py:329
  31.2 1.3 %fusion = (f32[1,256]{1,0:T(1,128)}, f32[1,256]{1,0:T(1,128)}) fusion(f32[2,256]{1,0:T(2,128)} %sinkhorn.1), kind=kLoop, calls=%fused_computation | loop fusion | bytes 4096 | tf_op jit(solution)/shard_map/slice | solution.py:366

commit v4 on v3

--- a/solution.py
+++ b/solution.py
@@ -162,6 +162,15 @@
         owner = lax.rem(me_r + n_r - k, n_r)
         row_copy(ref_of(owner), send, recv, k).wait_recv()
 
+    first = 1 + lax.rem(me_c, 2)
+    if relayed:
+        for h in range(mb):
+            s_arrive(first, h)
+
+            @pl.when(inner)
+            def _():
+                s_copy(first, 3 * me_c - 3, 2, h).start()
+
     @pl.when(odd == 1)
     def _():
         for copy in swaps:
@@ -182,40 +191,42 @@
         hit = jnp.where(live, 1.0, hit)
     mask[...] = hit
 
-    first = 1 + lax.rem(me_c, 2)
-    if relayed:
-        for h in range(mb):
-            s_arrive(first, h)
-
-            @pl.when(inner)
-            def _():
-                s_copy(first, 3 * me_c - 3, 2, h).start()
-
-    for k in range(1, n_r):
-        from_row(lambda o: tp.at[o], t_send.at[k - 1], t_recv.at[k - 1], k)
-
     ones = jnp.ones((16, T), jnp.bfloat16)
-    width = min(T, 1024)
     scale = math.log2(math.e) / strength
 
-    def build(owner, awaited=True):
-        for b in range(mb):
-            if awaited:
-                s_arrive(owner, b)
-            block = sp[owner, b * BS:(b + 1) * BS, :]
-            row0 = pl.multiple_of(owner * m + b * BS, BS)
-            for t0 in range(0, n_r):
-                sim = lax.dot_general(block, tp[t0], NT, preferred_element_type=jnp.float32)
-                live = mask[pl.ds(owner * mb + b, 1), t0 * m:(t0 + 1) * m]
-                gibbs[pl.ds(row0, BS), t0 * m:(t0 + 1) * m] = (
-                    jnp.exp2(sim * scale) * live).astype(jnp.bfloat16)
-        rows = pl.ds(pl.multiple_of(owner * m, m), m)
+    def tile(owner, b, t):
+        block = sp[owner, b * BS:(b + 1) * BS, :]
+        row0 = pl.multiple_of(owner * m + b * BS, BS)
+        columns = pl.ds(pl.multiple_of(t * m, m), m)
+        sim = lax.dot_general(block, tp[t], NT, preferred_element_type=jnp.float32)
+        live = mask[pl.ds(owner * mb + b, 1), columns]
+        gibbs[pl.ds(row0, BS), columns] = (jnp.exp2(sim * scale) * live).astype(jnp.bfloat16)
+
+    def row_total(owner, b):
+        rows = pl.ds(pl.multiple_of(owner * m + b * BS, BS), BS)
         total = lax.dot_general(ones, gibbs[rows, :], NT, preferred_element_type=jnp.float32)
         rbuf[0, me_c, :, rows] = total[:1]
 
-    build(me_c, awaited=False)
+    def build(owner):
+        for b in range(mb):
+            s_arrive(owner, b)
+            for t in range(n_r):
+                tile(owner, b, t)
+            row_total(owner, b)
+
+    here = (me_c, first) if relayed else (me_c,)
+    near_row = 3 - 2 * lax.rem(me_r, 2) if n_r == 4 else 1
+    for k in (0, near_row, 4 - near_row, 2) if n_r == 4 else range(n_r):
+        t = lax.rem(me_r + n_r - k, n_r)
+        if not (isinstance(k, int) and k == 0):
+            row_copy(tp.at[t], t_send.at[k - 1], t_recv.at[k - 1], k).wait_recv()
+        for owner in here:
+            for b in range(mb):
+                tile(owner, b, t)
+    for owner in here:
+        for b in range(mb):
+            row_total(owner, b)
     if relayed:
-        build(first, awaited=False)
         build(3 * lax.rem(me_c + 1, 2))
         build(to_col(2))
     else:

time: 32.7 us -> 32.2 us (0.985)
  Pallas kernels: 30.6 us -> 30.1 us
    pallas_call x1, Pallas kernels: 30.6 us -> 30.1 us  [per_device(): pl.pallas_call(functools.partial(kernel, n_r, n_c), out_shape=jax.ShapeDt...]
where the time goes in v4:
time: 32.2 us; the launch traced here: 32 us
  Pallas kernels  30.1 us (93%)
  local copies, waits for them, and re-layouts  1.32 us (4%)
  between operations  0.64 us (2%)
    pallas_call x1, Pallas kernels, per_device(): pl.pallas_call(functools.partial(kernel, n_r, n_c), out_shape=jax.ShapeDt...  30.1 us
    slice x1, local copies, waits for them, and re-layouts, per_device(): return (pots[0], pots[1])  1.32 us

profile of v4, /device:TPU:0, one launch (start us, length us, event | category | flops | bytes accessed | tf_op | source)
XLA Modules:
  0.0 32.0 jit_solution(8349983725576761066)
XLA Ops:
  0.6 30.1 %sinkhorn.1 = f32[2,256]{1,0:T(2,128)} custom-call(bf16[256,256]{1,0:T(8,128)(2,1)} %src_hbm.1, bf16[256,256]{1,0:T(8,128)(2,1)} %tgt_hbm.1, f32[1,256]{1,0:T(1,128)} %bitcast.7, f32[1,256]{1,0:T(1,128)} %bitcast.8, s32[4,8]{1,0:T(4,128)} %bitcast.6, s32[1,8]{1,0:T(1,128)} %bitcast.11), custom_call_target="tpu_custom_call" | custom-call | tf_op jit(solution)/shard_map/sinkhorn/pallas_call | solution.py:340
  30.7 1.3 %fusion = (f32[1,256]{1,0:T(1,128)}, f32[1,256]{1,0:T(1,128)}) fusion(f32[2,256]{1,0:T(2,128)} %sinkhorn.1), kind=kLoop, calls=%fused_computation | loop fusion | bytes 4096 | tf_op jit(solution)/shard_map/slice | solution.py:377

commit v5 on v4

--- a/solution.py
+++ b/solution.py
@@ -288,7 +288,14 @@
             pot_ref[0:1] = pout[...]
 
     def exchange_cols(it):
-        out = [row_copy(cbuf.at[it, me_r], c_send.at[it, k - 1], c_recv.at[it, k - 1], k)
+        final = it == ITERS - 1
+
+        def sums(o, reader):
+            if not final:
+                return cbuf.at[it, o]
+            return cbuf.at[it, o, :, pl.ds(pl.multiple_of(reader * m, m), m)]
+
+        out = [row_copy(sums(me_r, to_row(k)), c_send.at[it, k - 1], c_recv.at[it, k - 1], k)
                for k in range(1, n_r)]
         for copy in out:
             copy.start()
@@ -298,7 +305,9 @@
             for k in range(1, n_r):
                 from_row(lambda o: tm.at[o], tm_send.at[k - 1], tm_recv.at[k - 1], k)
         for k in range(1, n_r):
-            from_row(lambda o: cbuf.at[it, o], c_send.at[it, k - 1], c_recv.at[it, k - 1], k)
+            from_row(lambda o: sums(o, me_r), c_send.at[it, k - 1], c_recv.at[it, k - 1], k)
+        if final:
+            return out, None
         total = cbuf[it, 0]
         for j in range(1, n_r):
             total = total + cbuf[it, j]

time: 32.2 us -> 32.1 us (level)
  no operation moved by 1% of the time
where the time goes in v5:
time: 32.1 us; the launch traced here: 32 us
  Pallas kernels  30 us (93%)
  local copies, waits for them, and re-layouts  1.32 us (4%)
  between operations  0.64 us (2%)
    pallas_call x1, Pallas kernels, per_device(): pl.pallas_call(functools.partial(kernel, n_r, n_c), out_shape=jax.ShapeDt...  30 us
    slice x1, local copies, waits for them, and re-layouts, per_device(): return (pots[0], pots[1])  1.32 us

profile of v5, /device:TPU:0, one launch (start us, length us, event | category | flops | bytes accessed | tf_op | source)
XLA Modules:
  0.0 32.0 jit_solution(3354790302810664595)
XLA Ops:
  0.6 30.0 %sinkhorn.1 = f32[2,256]{1,0:T(2,128)} custom-call(bf16[256,256]{1,0:T(8,128)(2,1)} %src_hbm.1, bf16[256,256]{1,0:T(8,128)(2,1)} %tgt_hbm.1, f32[1,256]{1,0:T(1,128)} %bitcast.7, f32[1,256]{1,0:T(1,128)} %bitcast.8, s32[4,8]{1,0:T(4,128)} %bitcast.6, s32[1,8]{1,0:T(1,128)} %bitcast.11), custom_call_target="tpu_custom_call" | custom-call | tf_op jit(solution)/shard_map/sinkhorn/pallas_call | solution.py:349
  30.7 1.3 %fusion = (f32[1,256]{1,0:T(1,128)}, f32[1,256]{1,0:T(1,128)}) fusion(f32[2,256]{1,0:T(2,128)} %sinkhorn.1), kind=kLoop, calls=%fused_computation | loop fusion | bytes 4096 | tf_op jit(solution)/shard_map/slice | solution.py:386
